TPU v7x, 32 devices: a whole 2x2x4 slice. The times are simulated.
32 devices in a mesh: blocks: 8 (over z, x), cols: 4 (over y, core).
Axes of the slice: x: 2, y: 2, z: 4, core: 2. Of those that a mesh axis runs over, the one named last changes fastest.
Arguments:
- border: bfloat16 [512, 64, 2048], P('blocks', None, 'cols')
- block_inverse: bfloat16 [512, 64, 64], P('blocks'), as said below
- pattern: int32 [512, 32], P('blocks', 'cols'), may hold values 0 or 1
- rhs_blocks: float32 [512, 64], P('blocks'), may hold values from -6 to 6
- link_diag: float32 [2048], P('cols'), may hold values from 0.001 to 0.3
- link_rhs: float32 [2048], P('cols'), may hold values from -6 to 6
Outputs:
- block_step: float32 [512, 64], P('blocks')
- link_step: float32 [2048], P('cols')
Inputs may be any that keep to these rules, and one draw needn't show every extreme that they name: `block_inverse`: each 64 x 64 block is symmetric and positive definite.
All inputs are finite; a program needn't handle non-finite values. No bound on the sum of `pattern` on one device may be relied on, other than what follows from the above.
Results may differ from a plain program's by a relative error of at most 0.0024.
Values may be sent and summed in bfloat16 or wider, within the bound.
A program may use at most 128 MiB of HBM per device.

v0:
```python
import jax
import jax.numpy as jnp
from jax import lax
from jax.sharding import PartitionSpec as P


def apply_pattern(border, pattern):
    hours, order, width = border.shape
    panels = pattern.shape[1]
    shaped = border.reshape(hours, order, panels, width // panels)
    keep = pattern.astype(border.dtype)[:, None, :, None]
    return (shaped * keep).reshape(hours, order, width)


def blocked_solve(complement, right_side):
    extent = complement.shape[0]
    stride = min(512, extent)
    steps = extent // stride
    trailing = complement
    diagonals = []
    panels = []
    for level in range(steps):
        corner = jnp.linalg.cholesky(trailing[:stride, :stride])
        diagonals.append(corner)
        if level + 1 < steps:
            below = trailing[stride:, :stride]
            panel = jax.scipy.linalg.solve_triangular(corner, below.T, lower=True).T
            panels.append(panel)
            trailing = trailing[stride:, stride:] - jnp.dot(
                panel, panel.T, precision=lax.Precision.HIGHEST
            )
    forward = []
    remaining = right_side
    for level in range(steps):
        piece = jax.scipy.linalg.solve_triangular(diagonals[level], remaining[:stride], lower=True)
        forward.append(piece)
        if level + 1 < steps:
            remaining = remaining[stride:] - jnp.dot(
                panels[level], piece, precision=lax.Precision.HIGHEST
            )
    later = jnp.zeros((0,), jnp.float32)
    for level in range(steps - 1, -1, -1):
        target = forward[level]
        if level + 1 < steps:
            target = target - jnp.dot(panels[level].T, later, precision=lax.Precision.HIGHEST)
        piece = jax.scipy.linalg.solve_triangular(diagonals[level], target, lower=True, trans=1)
        later = jnp.concatenate([piece, later])
    return later


def per_device(border, block_inverse, pattern, rhs_blocks, link_diag, link_rhs):
    masked = apply_pattern(border, pattern)
    hours, order, own_width = masked.shape
    groups = lax.axis_size("cols")
    width = own_width * groups
    column = lax.axis_index("cols")
    offset = column * own_width
    inverse_wide = block_inverse.astype(jnp.float32)
    weighted = jnp.einsum("bij,bj->bi", inverse_wide, rhs_blocks, precision=lax.Precision.HIGHEST)
    weighted_low = weighted.astype(jnp.bfloat16)
    flat_masked = masked.reshape(hours * order, own_width)
    partial_rhs = jnp.dot(
        weighted_low.reshape(1, hours * order), flat_masked, preferred_element_type=jnp.float32
    )[0]
    contract = (((0,), (0,)), ((), ()))
    quarter = hours // groups
    mine = lax.all_to_all(masked, "cols", split_axis=0, concat_axis=2, tiled=True)
    inverse_mine = lax.dynamic_slice_in_dim(block_inverse, column * quarter, quarter, 0)
    solved_mine = jnp.einsum(
        "bij,bjk->bik", inverse_mine, mine, preferred_element_type=jnp.float32
    ).astype(jnp.bfloat16)
    flat_mine = mine.reshape(quarter * order, width)
    flat_solved = solved_mine.reshape(quarter * order, width)
    share = lax.psum_scatter(
        lax.dot_general(flat_solved, flat_mine, contract, preferred_element_type=jnp.float32),
        "cols",
        scatter_dimension=0,
        tiled=True,
    )
    levels = lax.axis_size("blocks")
    slab = own_width // levels
    place = lax.axis_index("blocks") * slab
    part_sum, part_rhs = (
        lax.psum_scatter(share, "blocks", scatter_dimension=0, tiled=True),
        lax.psum_scatter(partial_rhs, "blocks", scatter_dimension=0, tiled=True),
    )
    part_reduced = part_rhs - lax.dynamic_slice_in_dim(link_rhs, place, slab, 0)
    part_diag = lax.dynamic_slice_in_dim(link_diag, place, slab, 0)
    pieces, piece_rhs, piece_diag = (
        lax.all_gather(part_sum[None], ("blocks", "cols"), axis=0, tiled=True),
        lax.all_gather(part_reduced[None], ("blocks", "cols"), axis=0, tiled=True),
        lax.all_gather(part_diag[None], ("blocks", "cols"), axis=0, tiled=True),
    )
    whole = jnp.transpose(pieces.reshape(levels, groups, slab, width), (1, 0, 2, 3)).reshape(
        width, width
    )
    whole_rhs = jnp.transpose(piece_rhs.reshape(levels, groups, slab), (1, 0, 2)).reshape(width)
    whole_diag = jnp.transpose(piece_diag.reshape(levels, groups, slab), (1, 0, 2)).reshape(width)
    complement = jnp.diag(whole_diag) + 0.5 * (whole.T + whole)
    link_full = blocked_solve(complement, whole_rhs)
    link_low = link_full.astype(jnp.bfloat16)
    own_low = lax.dynamic_slice_in_dim(link_low, offset, own_width, 0)
    partial_coupling = jnp.dot(flat_masked, own_low, preferred_element_type=jnp.float32).reshape(
        hours, order
    )
    coupling = lax.psum(partial_coupling, "cols")
    block_step = jnp.einsum(
        "bij,bj->bi", inverse_wide, rhs_blocks - coupling, precision=lax.Precision.HIGHEST
    )
    return (block_step, lax.dynamic_slice_in_dim(link_full, offset, own_width, 0))


def solution(mesh):
    placed = (
        P("blocks", None, "cols"),
        P("blocks", None, None),
        P("blocks", "cols"),
        P("blocks", None),
        P("cols"),
        P("cols"),
    )
    return jax.shard_map(
        per_device,
        mesh=mesh,
        in_specs=placed,
        out_specs=(P("blocks", None), P("cols")),
        check_vma=False,
    )
```

profile of v0, /device:TPU:0, one launch (start us, length us, event | category | flops | bytes accessed | tf_op | source)
XLA Modules:
  0.0 1235.2 jit_solution(10031797152547322615)
XLA Ops:
  17.8 48.8 %all-to-all-done = bf16[64,64,512]{2,1,0:T(8,128)(2,1)} async-done(((bf16[64,64,512]{2,1,0:T(8,128)(2,1)}), bf16[64,64,512]{2,1,0:T(8,128)(2,1)}, u32[]{:S(2)}, u32[]{:S(2)}) %all-to-all-start) | async-done | bytes 4194336 | tf_op jit(solution)/shard_map/all_to_all | solution.py:67
  87.0 11.7 fusion.307
  98.8 127.4 %reduce-scatter.3.cloned.1.call-done = f32[512,2048]{1,0:T(8,128)} async-done(((f32[2048,2048]{1,0:T(8,128)}), f32[512,2048]{1,0:T(8,128)}) %reduce-scatter.3.cloned.1.call-update) | async-done | bytes 4194320 | tf_op jit(solution)/shard_map/reduce_scatter | solution.py:74
  226.3 91.9 %reduce-scatter.5.cloned.1.call-done = f32[64,2048]{1,0:T(8,128)} async-done(((f32[512,2048]{1,0:T(8,128)}), f32[64,2048]{1,0:T(8,128)}) %reduce-scatter.5.cloned.1.call-update) | async-done | bytes 524304 | tf_op jit(solution)/shard_map/reduce_scatter | solution.py:84
  324.0 20.2 %all-reduce.3 = f32[512]{0:T(512)S(1)} all-reduce(f32[512]{0:T(512)S(1)} %bitcast.729), channel_id=7, replica_groups=mesh['blocks'=8,'cols'=4] {'blocks'}, use_global_device_ids=true, to_apply=%region_10.12.clone | all-reduce | flops 512 | bytes 4096
  346.0 38.7 %all-reduce.4 = (f32[2048]{0:T(1024)S(1)}, f32[2048]{0:T(1024)S(1)}) all-reduce(f32[2048]{0:T(1024)S(1)} %dynamic-slice_dynamic-update-slice_fusion, f32[2048]{0:T(1024)S(1)} %fusion.254), channel_id=2, replica_groups=mesh['blocks'=8,'cols'=4] {'blocks','cols'}, use_global_device_ids=true, to_apply=%add.1 | all-reduce | flops 4096 | bytes 32768
  385.1 51.8 %all-gather.5.cloned.1.call-done = f32[2048,2048]{1,0:T(8,128)} async-done(((f32[64,2048]{1,0:T(8,128)}), f32[2048,2048]{1,0:T(8,128)}) %all-gather.5.cloned.1.call-update) | async-done | bytes 16777232 | tf_op jit(solution)/shard_map/all_gather | solution.py:90
  436.9 11.6 copy.46
  448.5 17.6 %copy.47 = f32[2048,2048]{0,1:T(8,128)} copy(f32[2048,2048]{1,0:T(8,128)} %bitcast.704) | data formatting | bytes 33554432 | tf_op jit(solution)/shard_map/reshape | solution.py:94
  466.1 12.1 fusion.1
  487.5 11.7 cholesky.462
  499.3 9.8 custom-call.56
  509.9 11.7 cholesky.481
  521.7 18.5 %custom-call.57 = f32[1,128,128]{1,2,0:T(8,128)S(1)} custom-call(f32[1,128,128]{2,1,0:T(8,128)S(1)} %get-tuple-element.173), custom_call_target="InvertDiagBlocksLowerTriangular" | custom-call | tf_op jit(solution)/shard_map/jit(cholesky)/cholesky | solution.py:23
  540.9 11.7 cholesky.502
  553.3 9.8 custom-call.58
  563.7 11.9 cholesky.519
  587.1 39.3 %custom-call.75 = f32[4,128,128]{1,2,0:T(8,128)S(1)} custom-call(f32[4,128,128]{2,1,0:T(8,128)S(1)} %get-tuple-element.88), custom_call_target="InvertDiagBlocksLowerTriangular" | custom-call | tf_op jit(solution)/shard_map/jit(_solve_triangular)/triangular_solve | solution.py:46
  636.6 18.6 %slice_subtract_fusion = f32[1536,1536]{0,1:T(8,128)S(1)} fusion(f32[2048,2048]{0,1:T(8,128)} %copy-done.2, f32[128,1536]{1,0:T(8,128)S(1)} %fusion.180, f32[128,1536]{1,0:T(8,128)S(1)} %fusion.179, f32[128,1536]{1,0:T(8,128)S(1)} %fusion.178, f32[128,1536]{1,0:T(8,128)S(1)} %fusion.83), kind=kOutput, calls=%fused_computation.12 | convolution fusion | flops 14500233216 | bytes 22020096 | tf_op jit(solution)/shard_map/dot_general | solution.py:29
  669.2 11.7 cholesky.534
  682.2 9.8 custom-call.60
  695.2 12.1 cholesky.553
  709.2 9.8 custom-call.61
  721.4 11.7 cholesky.574
  734.4 9.8 custom-call.62
  746.5 11.9 cholesky.591
  764.3 11.8 while.21
  776.1 39.3 %custom-call.74 = f32[4,128,128]{1,2,0:T(8,128)S(1)} custom-call(f32[4,128,128]{2,1,0:T(8,128)S(1)} %get-tuple-element.87), custom_call_target="InvertDiagBlocksLowerTriangular" | custom-call | tf_op jit(solution)/shard_map/jit(_solve_triangular)/triangular_solve | solution.py:46
  829.1 9.6 slice_subtract_fusion.1
  846.9 11.7 cholesky.606
  859.8 9.8 custom-call.64
  872.8 11.9 cholesky.625
  886.7 9.8 custom-call.65
  898.8 11.7 cholesky.646
  911.9 9.8 custom-call.66
  924.0 12.1 cholesky.663
  942.3 12.1 while.20
  955.1 40.1 %custom-call.73 = f32[4,128,128]{1,2,0:T(8,128)S(1)} custom-call(f32[4,128,128]{2,1,0:T(8,128)} %copy-done.34), custom_call_target="InvertDiagBlocksLowerTriangular" | custom-call | tf_op jit(solution)/shard_map/jit(_solve_triangular)/triangular_solve | solution.py:46
  1018.5 11.7 cholesky.678
  1032.0 10.0 custom-call.68
  1045.9 11.7 cholesky.697
  1060.1 9.8 custom-call.69
  1073.9 13.2 %cholesky.718 = f32[128,128]{1,0:T(8,128)} custom-call(f32[128,128]{1,0:T(8,128)} %cholesky.794), custom_call_target="Cholesky" | custom-call | tf_op jit(solution)/shard_map/jit(cholesky)/cholesky | solution.py:23
  1089.2 11.5 custom-call.70
  1103.8 11.7 cholesky.735
  1122.5 13.5 %while.19 = (s32[]{:T(128)}, f32[512,512]{1,0:T(8,128)}, s32[4,2]{0,1:T(2,128)S(1)}, f32[4,128,128]{2,1,0:T(8,128)}, s32[]{:T(128)}) while((s32[]{:T(128)}, f32[512,512]{1,0:T(8,128)}, s32[4,2]{0,1:T(2,128)S(1)}, f32[4,128,128]{2,1,0:T(8,128)}, s32[]{:T(128)}) %tuple.144), condition=%wide.while_cond.1, body=%wide.while_body.1.sunk | while | flops 2 | bytes 132705 | solution.py:46
  1136.0 41.0 %custom-call.72 = f32[4,128,128]{1,2,0:T(8,128)} custom-call(f32[4,128,128]{2,1,0:T(8,128)} %get-tuple-element.85), custom_call_target="InvertDiagBlocksLowerTriangular" | custom-call | tf_op jit(solution)/shard_map/jit(_solve_triangular)/triangular_solve | solution.py:46
  1214.3 11.5 psum.7
  (385 shorter events, 266.8 us)
Async XLA Ops:
  7.2 78.6 %copy-start = (bf16[64,64,64]{2,1,0:T(8,128)(2,1)S(1)}, bf16[64,64,64]{2,1,0:T(8,128)(2,1)}, u32[]{:S(2)}) copy-start(bf16[64,64,64]{2,1,0:T(8,128)(2,1)} %param.12) | copy-start | bytes 1572868
  12.9 53.7 %all-to-all-start = ((bf16[64,64,512]{2,1,0:T(8,128)(2,1)}), bf16[64,64,512]{2,1,0:T(8,128)(2,1)}, u32[]{:S(2)}, u32[]{:S(2)}) async-start(bf16[64,64,512]{2,1,0:T(8,128)(2,1)} %broadcast_multiply_fusion), calls=%async_computation | async-start | bytes 8388608 | tf_op jit(solution)/shard_map/all_to_all | solution.py:67
  17.7 208.5 %reduce-scatter.3.cloned.1.call-start = ((), (), s32[]{:S(2)}) async-start(), calls=%async_computation.3 | async-start | bytes 20971520 | tf_op jit(solution)/shard_map/reduce_scatter | solution.py:74
  82.0 3.8 copy-start.5
  98.8 219.5 %copy-start.50 = (u32[32]{0:T(128)S(1)}, u32[32]{0:T(128)}, u32[]{:S(2)}) copy-start(u32[32]{0:T(128)} %constant.278) | copy-start | bytes 388
  98.8 220.6 %copy-start.35 = (f32[64,64]{1,0:T(8,128)S(1)}, f32[64,64]{1,0:T(8,128)}, u32[]{:S(2)}) copy-start(f32[64,64]{1,0:T(8,128)} %param.14) | copy-start | bytes 49156
  98.8 219.4 %reduce-scatter.5.cloned.1.call-start = ((), (), s32[]{:S(2)}) async-start(), calls=%async_computation.4 | async-start | bytes 4718592 | tf_op jit(solution)/shard_map/reduce_scatter | solution.py:84
  226.2 210.6 %all-gather.5.cloned.1.call-start = ((), (), s32[]{:S(2)}) async-start(), calls=%async_computation.5 | async-start | bytes 17301504 | tf_op jit(solution)/shard_map/all_gather | solution.py:90
  478.2 5.7 copy-start.2
  587.1 41.5 %copy-start.12 = (f32[512,512]{1,0:T(8,128)}, f32[512,512]{1,0:T(8,128)S(1)}, u32[]{:S(2)}) copy-start(f32[512,512]{1,0:T(8,128)S(1)} %get-tuple-element.371) | copy-start | bytes 3145732
  626.4 35.4 %copy-start.22 = (f32[4,128,128]{1,2,0:T(8,128)}, f32[4,128,128]{1,2,0:T(8,128)S(1)}, u32[]{:S(2)}) copy-start(f32[4,128,128]{1,2,0:T(8,128)S(1)} %custom-call.75) | copy-start | bytes 786436
  626.4 4.9 copy-start.6
  634.1 27.9 %copy-start.10 = (f32[128,1536]{1,0:T(8,128)}, f32[128,1536]{1,0:T(8,128)S(1)}, u32[]{:S(2)}) copy-start(f32[128,1536]{1,0:T(8,128)S(1)} %fusion.179) | copy-start | bytes 2359300
  636.6 25.5 %copy-start.17 = (f32[128,1536]{1,0:T(8,128)}, f32[128,1536]{1,0:T(8,128)S(1)}, u32[]{:S(2)}) copy-start(f32[128,1536]{1,0:T(8,128)S(1)} %fusion.180) | copy-start | bytes 2359300
  655.2 3.9 copy-start.3
  661.2 5.3 copy-start.37
  661.6 4.9 copy-start.42
  662.1 4.4 copy-start.46
  815.4 13.0 %copy-start.24 = (f32[4,128,128]{1,2,0:T(8,128)}, f32[4,128,128]{1,2,0:T(8,128)S(1)}, u32[]{:S(2)}) copy-start(f32[4,128,128]{1,2,0:T(8,128)S(1)} %custom-call.74) | copy-start | bytes 786436
  815.4 8.3 copy-start.7
  817.0 21.7 %copy-start.39 = (f32[128,1]{0,1:T(1,128)}, f32[128,1]{0,1:T(1,128)S(1)}, u32[]{:S(2)}) copy-start(f32[128,1]{0,1:T(1,128)S(1)} %convolution_bitcast_fusion.39) | copy-start | bytes 1540
  818.4 20.4 %copy-start.44 = (f32[128,1]{0,1:T(1,128)}, f32[128,1]{0,1:T(1,128)S(1)}, u32[]{:S(2)}) copy-start(f32[128,1]{0,1:T(1,128)S(1)} %convolution_bitcast_fusion.37) | copy-start | bytes 1540
  819.8 19.0 %copy-start.48 = (f32[128,1]{0,1:T(1,128)}, f32[128,1]{0,1:T(1,128)S(1)}, u32[]{:S(2)}) copy-start(f32[128,1]{0,1:T(1,128)S(1)} %convolution_bitcast_fusion.36) | copy-start | bytes 1540
  823.8 15.0 %copy-start.8 = (f32[128,1024]{1,0:T(8,128)}, f32[128,1024]{1,0:T(8,128)S(1)}, u32[]{:S(2)}) copy-start(f32[128,1024]{1,0:T(8,128)S(1)} %fusion.181) | copy-start | bytes 1572868
  826.2 12.6 %copy-start.14 = (f32[128,1024]{1,0:T(8,128)}, f32[128,1024]{1,0:T(8,128)S(1)}, u32[]{:S(2)}) copy-start(f32[128,1024]{1,0:T(8,128)S(1)} %fusion.182) | copy-start | bytes 1572868
  829.1 9.7 copy-start.30
  995.2 4.1 copy-start.26
  999.4 5.7 copy-start.27
  1003.5 8.5 copy-start.16
  1005.5 7.1 copy-start.29
  1007.7 5.5 copy-start.32
  1119.3 75.0 %copy-start.40 = (f32[128,1]{0,1:T(1,128)S(1)}, f32[128,1]{0,1:T(1,128)}, u32[]{:S(2)}) copy-start(f32[128,1]{0,1:T(1,128)} %copy-done.39) | copy-start | bytes 1540
  1119.4 75.0 %copy-start.45 = (f32[128,1]{0,1:T(1,128)S(1)}, f32[128,1]{0,1:T(1,128)}, u32[]{:S(2)}) copy-start(f32[128,1]{0,1:T(1,128)} %copy-done.44) | copy-start | bytes 1540
  1119.4 75.0 %copy-start.49 = (f32[128,1]{0,1:T(1,128)S(1)}, f32[128,1]{0,1:T(1,128)}, u32[]{:S(2)}) copy-start(f32[128,1]{0,1:T(1,128)} %copy-done.48) | copy-start | bytes 1540
  1119.4 75.1 %copy-start.38 = (f32[128,1]{0,1:T(1,128)S(1)}, f32[128,1]{0,1:T(1,128)}, u32[]{:S(2)}) copy-start(f32[128,1]{0,1:T(1,128)} %copy-done.37) | copy-start | bytes 1540
  1119.4 75.1 %copy-start.43 = (f32[128,1]{0,1:T(1,128)S(1)}, f32[128,1]{0,1:T(1,128)}, u32[]{:S(2)}) copy-start(f32[128,1]{0,1:T(1,128)} %copy-done.42) | copy-start | bytes 1540
  1119.4 75.1 %copy-start.47 = (f32[128,1]{0,1:T(1,128)S(1)}, f32[128,1]{0,1:T(1,128)}, u32[]{:S(2)}) copy-start(f32[128,1]{0,1:T(1,128)} %copy-done.46) | copy-start | bytes 1540
  1119.4 75.1 %copy-start.41 = (f32[512,1]{0,1:T(1,128)S(1)}, f32[512,1]{0,1:T(1,128)}, u32[]{:S(2)}) copy-start(f32[512,1]{0,1:T(1,128)} %pad_maximum_fusion.17) | copy-start | bytes 6148
  1176.9 17.6 %copy-start.28 = (f32[4,128,128]{1,2,0:T(8,128)S(1)}, f32[4,128,128]{1,2,0:T(8,128)}, u32[]{:S(2)}) copy-start(f32[4,128,128]{1,2,0:T(8,128)} %copy-done.26) | copy-start | bytes 786436
  1176.9 21.8 %copy-start.9 = (f32[128,1024]{1,0:T(8,128)S(1)}, f32[128,1024]{1,0:T(8,128)}, u32[]{:S(2)}) copy-start(f32[128,1024]{1,0:T(8,128)} %copy-done.8) | copy-start | bytes 1572868
  1176.9 21.8 %copy-start.15 = (f32[128,1024]{1,0:T(8,128)S(1)}, f32[128,1024]{1,0:T(8,128)}, u32[]{:S(2)}) copy-start(f32[128,1024]{1,0:T(8,128)} %copy-done.14) | copy-start | bytes 1572868
  1177.0 21.8 %copy-start.31 = (f32[128,1024]{1,0:T(8,128)S(1)}, f32[128,1024]{1,0:T(8,128)}, u32[]{:S(2)}) copy-start(f32[128,1024]{1,0:T(8,128)} %copy-done.30) | copy-start | bytes 1572868
  1189.8 10.8 copy-start.25
  1192.1 12.9 %copy-start.11 = (f32[128,1536]{1,0:T(8,128)S(1)}, f32[128,1536]{1,0:T(8,128)}, u32[]{:S(2)}) copy-start(f32[128,1536]{1,0:T(8,128)} %copy-done.10) | copy-start | bytes 2359300
  1192.1 12.9 %copy-start.18 = (f32[128,1536]{1,0:T(8,128)S(1)}, f32[128,1536]{1,0:T(8,128)}, u32[]{:S(2)}) copy-start(f32[128,1536]{1,0:T(8,128)} %copy-done.17) | copy-start | bytes 2359300
  1200.6 7.2 copy-start.23
  1203.3 9.3 copy-start.1
  1207.7 18.1 %copy-start.36 = (f32[64,64]{1,0:T(8,128)S(1)}, f32[64,64]{1,0:T(8,128)}, u32[]{:S(2)}) copy-start(f32[64,64]{1,0:T(8,128)} %param.14) | copy-start | bytes 49156
  (7 other events, 10.7 us)
Sparse Core Ops, SparseCore 0:
  98.9 127.2 reduce-scatter.2
  230.2 87.8 reduce-scatter.4
  321.1 115.7 all-gather.4
where the time goes:
time: 1250 us; the launch traced here: 1240 us
  other arithmetic  530 us (42%)
  waiting for transfers between devices  320 us (26%)
  matrix products  157 us (13%)
  local copies, waits for them, and re-layouts  127 us (10%)
  blocking collectives  70.4 us (6%)
  between operations  26 us (2%)
    another operation x59, other arithmetic, blocked_solve(): corner = jnp.linalg.cholesky(trailing[:stride, :stride])  336 us
    another operation x13, other arithmetic, blocked_solve(): jax.scipy.linalg.solve_triangular(diagonals[level], target, lower=True, t...  167 us
    reduce_scatter x1, waiting for transfers between devices, per_device(): lax.psum_scatter(lax.dot_general(flat_solved, flat_mine, contract, prefer...  127 us
    reduce_scatter x1, waiting for transfers between devices, per_device(): lax.psum_scatter(share, 'blocks', scatter_dimension=0, tiled=True)  91.9 us
    unnamed x2, blocking collectives  58.9 us
    all_gather x1, waiting for transfers between devices, per_device(): lax.all_gather(part_sum[None], ('blocks', 'cols'), axis=0, tiled=True)  51.8 us
    all_to_all x1, waiting for transfers between devices, per_device(): lax.all_to_all(masked, 'cols', split_axis=0, concat_axis=2, tiled=True)  48.8 us
    another operation x53, local copies, waits for them, and re-layouts, blocked_solve(): jax.scipy.linalg.solve_triangular(diagonals[level], target, lower=True, t...  45.3 us
  transfers between devices with their start and end apart: 4, of which 4 were waited for; matrix products, arithmetic and copies ran while one was open for 1% of the time, Pallas kernels for 0%

commit v1 on v0

v1 whole, which is shorter than its diff:
```python
import functools
import jax
import jax.numpy as jnp
from jax import lax
from jax.experimental import pallas as pl
from jax.experimental.pallas import tpu as pltpu
from jax.sharding import PartitionSpec as P

BLOCK = 128
STRIP = 256


def apply_pattern(border, pattern):
    hours, order, width = border.shape
    panels = pattern.shape[1]
    shaped = border.reshape(hours, order, panels, width // panels)
    keep = pattern.astype(border.dtype)[:, None, :, None]
    return (shaped * keep).reshape(hours, order, width)


def split_three(value):
    high = value.astype(jnp.bfloat16)
    rest = value - high.astype(jnp.float32)
    middle = rest.astype(jnp.bfloat16)
    low = (rest - middle.astype(jnp.float32)).astype(jnp.bfloat16)
    return high, middle, low


def invert_block(block_ref, order):
    groups = order // 8
    lane = lax.broadcasted_iota(jnp.int32, (8, order), 1)
    sub = lax.broadcasted_iota(jnp.int32, (8, order), 0)
    for group in range(groups):
        first = 8 * group
        inside = (lane >= first) & (lane < first + 8)
        own = block_ref[first : first + 8, :]
        corner = [jnp.broadcast_to(own[:, first + j : first + j + 1], (8, order)) for j in range(8)]
        own = jnp.where(inside, (lane == sub + first).astype(jnp.float32), own)
        for j in range(8):
            scale = 1.0 / corner[j][j : j + 1, :]
            factor = corner[j]
            row = own[j : j + 1, :] * scale
            own = jnp.where(sub == j, row, own - factor * row)
            for other in range(j + 1, 8):
                row = corner[other][j : j + 1, :] * scale
                corner[other] = jnp.where(sub == j, row, corner[other] - factor * row)
        for other in range(groups):
            if other == group:
                continue
            at = 8 * other
            theirs = block_ref[at : at + 8, :]
            total = jnp.where(inside, 0.0, theirs)
            for j in range(8):
                total = total - jnp.broadcast_to(theirs[:, first + j : first + j + 1], (8, order)) * own[j : j + 1, :]
            block_ref[at : at + 8, :] = total
        block_ref[first : first + 8, :] = own


def factor_kernel(extent, packed_ref, diag_ref, rhs_ref, out_ref, a_ref, left_ref, right_ref, rows_ref, wide_ref, block_ref, sems):
    nb, tile = BLOCK, STRIP
    strips = extent // tile
    steps = extent // nb
    per = tile // nb
    copies = []
    for strip in range(strips):
        fold = min(strip, strips - 1 - strip)
        start = 0 if strip == fold else (fold + 1) * tile
        width = (strip + 1) * tile
        copy = pltpu.make_async_copy(
            packed_ref.at[fold * tile : (fold + 1) * tile, start : start + width],
            a_ref.at[strip * tile : (strip + 1) * tile, 0:width],
            sems.at[strip],
        )
        copy.start()
        copies.append(copy)
    rows_ref[...] = jnp.broadcast_to(rhs_ref[...], rows_ref.shape)
    for copy in copies:
        copy.wait()
    eye = lax.broadcasted_iota(jnp.int32, (nb, nb), 0) == lax.broadcasted_iota(jnp.int32, (nb, nb), 1)
    nt = (((1,), (1,)), ((), ()))

    def forward(step, carry):
        base = pl.multiple_of(step * nb, nb)
        block_ref[...] = a_ref[pl.ds(base, nb), pl.ds(base, nb)] + jnp.where(eye, diag_ref[:, pl.ds(base, nb)], 0.0)
        invert_block(block_ref, nb)
        inverse = block_ref[...]
        a_ref[pl.ds(base, nb), pl.ds(base, nb)] = inverse
        first_tile = (step + 1) // per

        def panel(index, carry):
            at = pl.multiple_of(index * tile, tile)
            column = a_ref[pl.ds(at, tile), pl.ds(base, nb)]
            row_id = at + lax.broadcasted_iota(jnp.int32, (tile, nb), 0)
            column = jnp.where(row_id >= base + nb, column, 0.0)
            solved = jnp.dot(column, inverse, precision=lax.Precision.HIGHEST, preferred_element_type=jnp.float32)
            high, middle, low = split_three(column)
            left_ref[pl.ds(at, tile), :] = jnp.concatenate([high, high, middle, high, low, middle], axis=1)
            high, middle, low = split_three(solved)
            right_ref[pl.ds(at, tile), :] = jnp.concatenate([high, middle, high, low, high, middle], axis=1)
            return carry

        lax.fori_loop(first_tile, strips, panel, 0)
        high, middle, low = split_three(rows_ref[:, pl.ds(base, nb)])
        lead = jnp.concatenate([high, high, middle, high, low, middle], axis=1)

        def outer(index, carry):
            at = pl.multiple_of(index * tile, tile)
            theirs = right_ref[pl.ds(at, tile), :]
            rows_ref[:, pl.ds(at, tile)] -= lax.dot_general(lead, theirs, nt, preferred_element_type=jnp.float32)

            def inner(other, carry):
                to = pl.multiple_of(other * tile, tile)
                a_ref[pl.ds(to, tile), pl.ds(at, tile)] -= lax.dot_general(
                    left_ref[pl.ds(to, tile), :], theirs, nt, preferred_element_type=jnp.float32
                )
                return carry

            return lax.fori_loop(index, strips, inner, carry)

        return lax.fori_loop(first_tile, strips, outer, carry)

    lax.fori_loop(0, steps, forward, 0)

    def backward(count, carry):
        step = steps - 1 - count
        base = pl.multiple_of(step * nb, nb)

        def gather(index, total):
            at = pl.multiple_of(index * nb, nb)
            part = a_ref[pl.ds(at, nb), pl.ds(base, nb)] * wide_ref[pl.ds(at, nb), :]
            return total + jnp.sum(part.reshape(nb // 8, 8, nb), axis=0)

        total = lax.fori_loop(step + 1, steps, gather, jnp.zeros((8, nb), jnp.float32))
        target = rows_ref[0:1, pl.ds(base, nb)] - jnp.sum(total, axis=0, keepdims=True)
        tall = jnp.transpose(jnp.broadcast_to(target, (nb, nb)))
        piece = jnp.sum(a_ref[pl.ds(base, nb), pl.ds(base, nb)] * tall, axis=0, keepdims=True)
        out_ref[:, pl.ds(base, nb)] = piece
        wide_ref[pl.ds(base, nb), :] = jnp.transpose(jnp.broadcast_to(piece, (nb, nb)))
        return carry

    lax.fori_loop(0, steps, backward, 0)


def solve_packed(packed, diag, rhs):
    extent = diag.shape[0]
    out = pl.pallas_call(
        functools.partial(factor_kernel, extent),
        out_shape=jax.ShapeDtypeStruct((1, extent), jnp.float32),
        in_specs=[
            pl.BlockSpec(memory_space=pl.ANY),
            pl.BlockSpec(memory_space=pltpu.VMEM),
            pl.BlockSpec(memory_space=pltpu.VMEM),
        ],
        out_specs=pl.BlockSpec(memory_space=pltpu.VMEM),
        scratch_shapes=[
            pltpu.VMEM((extent, extent), jnp.float32),
            pltpu.VMEM((extent, 6 * BLOCK), jnp.bfloat16),
            pltpu.VMEM((extent, 6 * BLOCK), jnp.bfloat16),
            pltpu.VMEM((16, extent), jnp.float32),
            pltpu.VMEM((extent, BLOCK), jnp.float32),
            pltpu.VMEM((BLOCK, BLOCK), jnp.float32),
            pltpu.SemaphoreType.DMA((extent // STRIP,)),
        ],
        compiler_params=pltpu.CompilerParams(vmem_limit_bytes=40 * 1024 * 1024),
    )(packed, diag.reshape(1, extent), rhs.reshape(1, extent))
    return out[0]


def per_device(border, block_inverse, pattern, rhs_blocks, link_diag, link_rhs):
    masked = apply_pattern(border, pattern)
    hours, order, own_width = masked.shape
    groups = lax.axis_size("cols")
    width = own_width * groups
    column = lax.axis_index("cols")
    offset = column * own_width
    inverse_wide = block_inverse.astype(jnp.float32)
    weighted = jnp.einsum("bij,bj->bi", inverse_wide, rhs_blocks, precision=lax.Precision.HIGHEST)
    weighted_low = weighted.astype(jnp.bfloat16)
    flat_masked = masked.reshape(hours * order, own_width)
    partial_rhs = jnp.dot(
        weighted_low.reshape(1, hours * order), flat_masked, preferred_element_type=jnp.float32
    )[0]
    contract = (((0,), (0,)), ((), ()))
    quarter = hours // groups
    mine = lax.all_to_all(masked, "cols", split_axis=0, concat_axis=2, tiled=True)
    inverse_mine = lax.dynamic_slice_in_dim(block_inverse, column * quarter, quarter, 0)
    solved_mine = jnp.einsum(
        "bij,bjk->bik", inverse_mine, mine, preferred_element_type=jnp.float32
    ).astype(jnp.bfloat16)
    flat_mine = mine.reshape(quarter * order, width)
    flat_solved = solved_mine.reshape(quarter * order, width)
    strips = width // STRIP
    left = jnp.concatenate([flat_mine, flat_solved], axis=0)
    right = jnp.concatenate([flat_solved, flat_mine], axis=0)
    bands = [
        0.5
        * lax.dot_general(
            left[:, s * STRIP : (s + 1) * STRIP],
            right[:, : (s + 1) * STRIP],
            contract,
            preferred_element_type=jnp.float32,
        )
        for s in range(strips)
    ]
    folded = jnp.concatenate(
        [jnp.concatenate([bands[s], bands[strips - 1 - s]], axis=1) for s in range(strips // 2)], axis=0
    )
    share = lax.psum_scatter(folded, "cols", scatter_dimension=0, tiled=True)
    part_sum = lax.psum_scatter(share, "blocks", scatter_dimension=0, tiled=True)
    packed = lax.all_gather(part_sum, ("cols", "blocks"), axis=0, tiled=True)
    own_rhs = lax.psum(partial_rhs, "blocks") - link_rhs
    vectors = lax.all_gather(jnp.stack([own_rhs, link_diag])[None], "cols", axis=0, tiled=True)
    vectors = jnp.transpose(vectors, (1, 0, 2)).reshape(2, width)
    link_full = solve_packed(packed, vectors[1], vectors[0])
    link_low = link_full.astype(jnp.bfloat16)
    own_low = lax.dynamic_slice_in_dim(link_low, offset, own_width, 0)
    partial_coupling = jnp.dot(flat_masked, own_low, preferred_element_type=jnp.float32).reshape(
        hours, order
    )
    coupling = lax.psum(partial_coupling, "cols")
    block_step = jnp.einsum(
        "bij,bj->bi", inverse_wide, rhs_blocks - coupling, precision=lax.Precision.HIGHEST
    )
    return (block_step, lax.dynamic_slice_in_dim(link_full, offset, own_width, 0))


def solution(mesh):
    placed = (
        P("blocks", None, "cols"),
        P("blocks", None, None),
        P("blocks", "cols"),
        P("blocks", None),
        P("cols"),
        P("cols"),
    )
    return jax.shard_map(
        per_device,
        mesh=mesh,
        in_specs=placed,
        out_specs=(P("blocks", None), P("cols")),
        check_vma=False,
    )
```

time: 1250 us -> 536 us (0.43); the launches traced: 1240 us -> 535 us
  other arithmetic: 530 us -> 11 us
  Pallas kernels: 0 us -> 167 us
  matrix products: 157 us -> 22.6 us
  local copies, waits for them, and re-layouts: 127 us -> 23.4 us
  waiting for transfers between devices: 320 us -> 256 us
  blocking collectives: 70.4 us -> 36 us
    another operation x76 -> x0, other arithmetic: 504 us -> none  [the longest x59 336 us: blocked_solve(): corner = jnp.linalg.cholesky(trailing[:stride, :stride])]
    pallas_call x0 -> x1, Pallas kernels: none -> 167 us  [solve_packed(): pl.pallas_call(functools.partial(factor_kernel, extent), out_shape=jax.Sh...]
    another operation x101 -> x0, matrix products: 92 us -> none  [the longest x21 27.5 us: blocked_solve(): panel = jax.scipy.linalg.solve_triangular(corner, below.T, lower=True).T]
    unnamed x2 -> x0, blocking collectives: 58.9 us -> none
    another operation x69 -> x0, local copies, waits for them, and re-layouts: 49.6 us -> none  [the longest x53 45.3 us: blocked_solve(): jax.scipy.linalg.solve_triangular(diagonals[level], target, lower=True, t...]
    reduce_scatter x1, waiting for transfers between devices: 127 us -> 79.7 us  [per_device(): share = lax.psum_scatter(folded, 'cols', scatter_dimension=0, tiled=True)]
    dot_general x10 -> x8, matrix products: 54.7 us -> 12.7 us  [per_device(): lax.dot_general(left[:, s * STRIP:(s + 1) * STRIP], right[:, :(s + 1) * S...]
    reshape x4 -> x0, local copies, waits for them, and re-layouts: 29.4 us -> none  [the longest x1 17.6 us: per_device(): jnp.transpose(pieces.reshape(levels, groups, slab, width), (1, 0, 2, 3))]
where the time goes in v1:
time: 536 us; the launch traced here: 535 us
  waiting for transfers between devices  256 us (48%)
  Pallas kernels  167 us (31%)
  blocking collectives  36 us (7%)
  local copies, waits for them, and re-layouts  23.4 us (4%)
  matrix products  22.6 us (4%)
  between operations  13.9 us (3%)
  other arithmetic  11 us (2%)
    pallas_call x1, Pallas kernels, solve_packed(): pl.pallas_call(functools.partial(factor_kernel, extent), out_shape=jax.Sh...  167 us
    reduce_scatter x1, waiting for transfers between devices, per_device(): share = lax.psum_scatter(folded, 'cols', scatter_dimension=0, tiled=True)  79.7 us
    reduce_scatter x1, waiting for transfers between devices, per_device(): lax.psum_scatter(share, 'blocks', scatter_dimension=0, tiled=True)  72.5 us
    all_gather x1, waiting for transfers between devices, per_device(): packed = lax.all_gather(part_sum, ('cols', 'blocks'), axis=0, tiled=True)  54.9 us
    all_to_all x1, waiting for transfers between devices, per_device(): lax.all_to_all(masked, 'cols', split_axis=0, concat_axis=2, tiled=True)  48.7 us
    psum x1, blocking collectives, per_device(): own_rhs = lax.psum(partial_rhs, 'blocks') - link_rhs  19.3 us
    all_to_all x2, local copies, waits for them, and re-layouts, per_device(): lax.all_to_all(masked, 'cols', split_axis=0, concat_axis=2, tiled=True)  15.5 us
    dot_general x8, matrix products, per_device(): lax.dot_general(left[:, s * STRIP:(s + 1) * STRIP], right[:, :(s + 1) * S...  12.7 us
  transfers between devices with their start and end apart: 4, of which 4 were waited for; matrix products, arithmetic and copies ran while one was open for 1% of the time, Pallas kernels for 0%

profile of v1, /device:TPU:0, one launch (start us, length us, event | category | flops | bytes accessed | tf_op | source)
XLA Modules:
  0.0 535.1 jit_solution(14095883245929463055)
XLA Ops:
  7.2 0.0 copy-start
  7.2 0.8 convert_element_type.14
  8.0 0.1 copy.11
  8.1 0.1 mul.70
  8.2 0.1 mul.71
  8.3 4.4 broadcast_multiply_fusion
  12.8 4.9 all-to-all-start
  17.7 0.0 reduce-scatter.3.cloned.1.call-start
  17.8 48.7 %all-to-all-done = bf16[64,64,512]{2,1,0:T(8,128)(2,1)} async-done(((bf16[64,64,512]{2,1,0:T(8,128)(2,1)}), bf16[64,64,512]{2,1,0:T(8,128)(2,1)}, u32[]{:S(2)}, u32[]{:S(2)}) %all-to-all-start) | async-done | bytes 4194336 | tf_op jit(solution)/shard_map/all_to_all | solution.py:185
  66.5 7.7 %copy.26 = bf16[4,16,64,512]{3,0,2,1:T(4,128)(2,1)} copy(bf16[4,16,64,512]{3,2,1,0:T(8,128)(2,1)} %bitcast) | data formatting | bytes 8388608 | tf_op jit(solution)/shard_map/all_to_all | solution.py:185
  74.2 7.8 %all_to_all.16 = bf16[16,64,2048]{2,1,0:T(8,128)(2,1)} reshape(bf16[16,64,4,512]{3,2,1,0:T(4,128)(2,1)} %bitcast.58) | data formatting | bytes 8388608 | tf_op jit(solution)/shard_map/all_to_all | solution.py:185
  82.0 3.7 copy.21
  85.7 0.0 copy-done
  85.8 0.0 copy-done.3
  85.8 1.2 convolution_convert_fusion
  87.0 2.3 fusion.25
  89.4 0.5 convolution_multiply_fusion
  89.9 0.7 fusion.35
  90.6 2.1 fusion.22
  92.8 1.0 fusion.32
  93.8 1.8 fusion.19
  95.6 1.3 fusion.29
  96.9 2.9 fusion.16
  99.8 5.8 %maximum_maximum_fusion = f32[1024,2304]{1,0:T(8,128)} fusion(f32[256,1280]{1,0:T(8,128)} %fusion.16, f32[256,1024]{1,0:T(8,128)S(1)} %fusion.29, f32[256,1536]{1,0:T(8,128)S(1)} %fusion.19, f32[256,768]{1,0:T(8,128)S(1)} %fusion.32, f32[256,1792]{1,0:T(8,128)S(1)} %fusion.22, f32[256,512]{1,0:T(8,128)S(1)} %fusion.35, f32[256,2048]{1,0:T(8,128)S(1)} %fusion.25, ...), kind=kLoop, calls=%fused_computation.27 | loop fusion | flops 16515072 | bytes 18874368 | tf_op jit(solution)/shard_map/concatenate | solution.py:205
  105.6 0.0 reduce-scatter.3.cloned.1.call-update
  105.6 0.0 copy-start.6
  105.6 0.0 copy-start.7
  105.6 0.0 reduce-scatter.5.cloned.1.call-start
  105.7 79.7 %reduce-scatter.3.cloned.1.call-done = f32[256,2304]{1,0:T(8,128)} async-done(((f32[1024,2304]{1,0:T(8,128)}), f32[256,2304]{1,0:T(8,128)}) %reduce-scatter.3.cloned.1.call-update) | async-done | bytes 2359312 | tf_op jit(solution)/shard_map/reduce_scatter | solution.py:208
  185.4 0.0 reduce-scatter.5.cloned.1.call-update
  185.4 0.0 all-gather.4.cloned.1.call-start
  185.4 72.5 %reduce-scatter.5.cloned.1.call-done = f32[32,2304]{1,0:T(8,128)} async-done(((f32[256,2304]{1,0:T(8,128)}), f32[32,2304]{1,0:T(8,128)}) %reduce-scatter.5.cloned.1.call-update) | async-done | bytes 294928 | tf_op jit(solution)/shard_map/reduce_scatter | solution.py:209
  257.9 0.0 all-gather.4.cloned.1.call-update
  257.9 0.0 copy-done.4
  258.0 1.7 fusion.73
  259.7 2.9 fusion.57
  262.6 19.3 %psum.14 = f32[512]{0:T(512)S(1)} all-reduce(f32[512]{0:T(512)S(1)} %bitcast.66), channel_id=1, replica_groups=mesh['blocks'=8,'cols'=4] {'blocks'}, use_global_device_ids=true, to_apply=%region_2.0 | all-reduce | flops 512 | bytes 4096 | tf_op jit(solution)/shard_map/psum | solution.py:211
  281.9 0.0 copy-done.6
  281.9 5.2 all-gather.1
  287.1 54.9 %all-gather.4.cloned.1.call-done.packed_ref = f32[1024,2304]{1,0:T(8,128)} async-done(((f32[32,2304]{1,0:T(8,128)}), f32[1024,2304]{1,0:T(8,128)}) %all-gather.4.cloned.1.call-update) | async-done | bytes 9437200 | tf_op jit(solution)/shard_map/all_gather | solution.py:210
  342.0 3.7 copy-done.1
  345.7 167.3 %shard_map.77 = f32[1,2048]{1,0:T(1,128)S(1)} custom-call(f32[1024,2304]{1,0:T(8,128)S(1)} %copy-done.1, f32[1,2048]{1,0:T(1,128)S(1)} %bitcast.41, f32[1,2048]{1,0:T(1,128)S(1)} %bitcast.40), custom_call_target="tpu_custom_call" | custom-call | tf_op jit(solution)/shard_map/pallas_call | solution.py:146
  513.0 0.0 copy-done.2
  513.0 0.0 copy-start.5
  513.0 1.7 fusion.59
  514.7 11.5 %psum.15 = f32[64,64]{1,0:T(8,128)S(1)} all-reduce(f32[64,64]{1,0:T(8,128)S(1)} %bitcast.60), channel_id=1, replica_groups=mesh['blocks'=8,'cols'=4] {'cols'}, use_global_device_ids=true, to_apply=%region_3.0 | all-reduce | flops 4096 | bytes 32768 | tf_op jit(solution)/shard_map/psum | solution.py:220
  526.3 2.4 fusion.74
  528.6 0.0 copy-done.5
  (11 shorter events, 0.1 us)
Async XLA Ops:
  7.2 78.6 %copy-start = (bf16[64,64,64]{2,1,0:T(8,128)(2,1)S(1)}, bf16[64,64,64]{2,1,0:T(8,128)(2,1)}, u32[]{:S(2)}) copy-start(bf16[64,64,64]{2,1,0:T(8,128)(2,1)} %param.7) | copy-start | bytes 1572868
  12.8 53.7 %all-to-all-start = ((bf16[64,64,512]{2,1,0:T(8,128)(2,1)}), bf16[64,64,512]{2,1,0:T(8,128)(2,1)}, u32[]{:S(2)}, u32[]{:S(2)}) async-start(bf16[64,64,512]{2,1,0:T(8,128)(2,1)} %broadcast_multiply_fusion), calls=%async_computation | async-start | bytes 8388608 | tf_op jit(solution)/shard_map/all_to_all | solution.py:185
  17.7 167.7 %reduce-scatter.3.cloned.1.call-start = ((), (), s32[]{:S(2)}) async-start(), calls=%async_computation.3 | async-start | bytes 11796480 | tf_op jit(solution)/shard_map/reduce_scatter | solution.py:208
  82.0 3.8 copy-start.3
  105.6 152.4 %copy-start.4 = (f32[64,64]{1,0:T(8,128)S(1)}, f32[64,64]{1,0:T(8,128)}, u32[]{:S(2)}) copy-start(f32[64,64]{1,0:T(8,128)} %param.9) | copy-start | bytes 49156
  105.6 176.3 %copy-start.6 = (f32[512]{0:T(512)S(1)}, f32[512]{0:T(512)}, u32[]{:S(2)}) copy-start(f32[512]{0:T(512)} %param.11) | copy-start | bytes 6148
  105.6 176.3 %copy-start.7 = (f32[512]{0:T(512)S(1)}, f32[512]{0:T(512)}, u32[]{:S(2)}) copy-start(f32[512]{0:T(512)} %param.10) | copy-start | bytes 6148
  105.6 152.3 %reduce-scatter.5.cloned.1.call-start = ((), (), s32[]{:S(2)}) async-start(), calls=%async_computation.4 | async-start | bytes 2654208 | tf_op jit(solution)/shard_map/reduce_scatter | solution.py:209
  185.4 156.6 %all-gather.4.cloned.1.call-start = ((), (), s32[]{:S(2)}) async-start(), calls=%async_computation.5 | async-start | bytes 9732096 | tf_op jit(solution)/shard_map/all_gather | solution.py:210
  342.0 3.7 copy-start.1
  345.7 167.3 %copy-start.2 = (bf16[64,64,512]{2,1,0:T(8,128)(2,1)S(1)}, bf16[64,64,512]{2,1,0:T(8,128)(2,1)}, u32[]{:S(2)}) copy-start(bf16[64,64,512]{2,1,0:T(8,128)(2,1)} %broadcast_multiply_fusion) | copy-start | bytes 12582916
  513.0 15.6 %copy-start.5 = (f32[1,512]{1,0:T(1,128)}, f32[1,512]{1,0:T(1,128)S(1)}, u32[]{:S(2)}) copy-start(f32[1,512]{1,0:T(1,128)S(1)} %constant_dynamic-slice_fusion) | copy-start | bytes 6148
Sparse Core Ops, SparseCore 0:
  105.7 79.5 reduce-scatter.2
  188.9 69.0 reduce-scatter.4
  260.9 81.0 all-gather.3
